TPU v7x, 32 devices: a whole 2x2x4 slice. The times are simulated.
32 devices in a mesh: groups: 2 (over x), row: 16 (over z, y, core).
Axes of the slice: x: 2, y: 2, z: 4, core: 2. Of those that a mesh axis runs over, the one named last changes fastest.
Arguments:
- basis: float32 [8192, 128], P(('groups', 'row')), parts along dimension 0, may hold values from -6 to 6
- springs: float32 [8192], P(('groups', 'row')), parts along dimension 0, may hold values from 0.25 to 8
- tangent_blocks: float32 [4096, 4096], P(('groups', 'row')), parts along dimension 0, may hold values from -0.375 to 0.375
- tile_rows: int32 [4096], P(('groups', 'row')), parts along dimension 0, may hold values from 0 to 3
- tile_owner: int32 [4096, 1], P(('groups', 'row')), parts along dimension 0, may hold values from 0 to 15, as said below
- tile_offset: int32 [4096], P(('groups', 'row')), parts along dimension 0, may hold values from 0 to 3
- tile_count: int32 [32], P(('groups', 'row')), parts along dimension 0, may hold values from 32 to 128, as said below
Outputs:
- stiff_image: float32 [8192, 128], P(('groups', 'row')), parts along dimension 0
- reduced: float32 [256, 128], P('groups'), parts along dimension 0
There are 2 independent parts, one for each index of `groups`. A program takes and returns all parts, laid end to end along the dimension named above; each array names one. Nothing has to cross between parts.
Inputs may be any that keep to these rules, and one draw needn't show every extreme that they name: The first tile_count[d] slots of device d are live; some device has exactly 128. `tile_owner`: the slab is closed into a shell: every slot of device d names owner (d + o) mod 16 with o one of 0, 1, -1, 4, -4, 5, -5, 8. Among the slots of one device no owner appears more than 32 times, and owner d itself appears exactly 32 times in every device.
All inputs are finite; a program needn't handle non-finite values.
Results may differ from a plain program's by a relative error of at most 0.0003.
Values sent between devices are 32-bit elements; how exact they have to be, the bound alone decides.
A program may use at most 128 MiB of HBM per device.

v0:
```python
import jax
import jax.numpy as jnp
from jax import lax
from jax.sharding import PartitionSpec as P

B = 64
MODES = 128
BR_DEV = 4
CAP = 128


def shards(basis, springs, tangent_blocks, tile_rows, tile_owner, tile_offset, tile_count):
    row_devices = lax.axis_size("row")
    dof_total = basis.shape[0] * row_devices
    own_blocks = basis.reshape(BR_DEV, B, MODES)
    square_blocks = tangent_blocks.reshape(CAP, B, B)
    owner_ids = tile_owner[:, 0]
    gathered = lax.all_gather(own_blocks, "row", axis=0, tiled=True)
    picked = gathered[owner_ids * BR_DEV + tile_offset]
    live_slot = (jnp.arange(CAP, dtype=jnp.int32) < tile_count[0]).astype(jnp.float32)
    row_ids = jnp.arange(BR_DEV, dtype=jnp.int32)
    products = jnp.einsum("sij,sjk->sik", square_blocks, picked, precision=lax.Precision.HIGHEST)
    row_select = (tile_rows[None, :] == row_ids[:, None]).astype(jnp.float32) * live_slot[None, :]
    summed = jnp.dot(row_select, products.reshape(CAP, B * MODES), precision=lax.Precision.HIGHEST)
    stiff_image = springs[:, None] * basis + summed.reshape(BR_DEV * B, MODES)
    partial_term = (
        jnp.einsum("rm,rn->mn", basis, stiff_image, precision=lax.Precision.HIGHEST) / dof_total
    )
    reduced = lax.psum(partial_term, "row")
    return (stiff_image, reduced)


def solution(mesh):
    in_specs = (
        P(("groups", "row"), None),
        P(("groups", "row")),
        P(("groups", "row"), None),
        P(("groups", "row")),
        P(("groups", "row"), None),
        P(("groups", "row")),
        P(("groups", "row")),
    )
    out_specs = (P(("groups", "row"), None), P("groups", None))
    return jax.shard_map(shards, mesh=mesh, in_specs=in_specs, out_specs=out_specs, check_vma=False)
```

profile of v0, /device:TPU:8, one launch (start us, length us, event | category | flops | bytes accessed | tf_op | source)
XLA Modules:
  0.0 163.7 jit_solution(6896301566178183216)
XLA Ops:
  7.2 0.0 all-gather.2.cloned.1.call-start
  7.2 0.7 all-gather.2.cloned.1.call-update
  7.9 0.0 all-reduce.2.cloned.1.call-start
  7.9 1.9 %copy.13 = f32[128,4096]{0,1:T(8,128)S(1)} copy(f32[128,4096]{1,0:T(8,128)} %param.9) | data formatting | bytes 4194304 | tf_op args[2]
  9.9 0.0 copy-start.4
  9.9 0.0 copy-start.5
  9.9 4.5 %copy.14 = f32[128,64,64]{2,1,0:T(8,128)} copy(f32[128,64,64]{0,2,1:T(8,128)S(1)} %bitcast.20) | data formatting | bytes 4194304 | tf_op jit(solution)/shard_map/reshape | solution.py:16
  15.1 0.0 copy-done.4
  15.1 0.0 copy-done.5
  15.1 36.7 %all-gather.2.cloned.1.call-done = f32[64,64,128]{2,1,0:T(8,128)} async-done(((f32[4,64,128]{2,1,0:T(8,128)}), f32[64,64,128]{2,1,0:T(8,128)}) %all-gather.2.cloned.1.call-update) | async-done | bytes 2097168 | tf_op jit(solution)/shard_map/all_gather | solution.py:18
  51.8 4.4 %gather_fusion = f32[128,64,128]{2,1,0:T(8,128)} fusion(f32[64,64,128]{2,1,0:T(8,128)} %all-gather.2.cloned.1.call-done, s32[1024]{0:T(1024)S(1)} %pad_clamp_fusion), kind=kCustom, calls=%fused_computation | custom fusion | bytes 8389120 | tf_op jit(solution)/shard_map/gather | solution.py:19
  56.1 6.5 %fusion.9 = f32[128,128,64]{1,2,0:T(8,128)S(1)} fusion(f32[128,64,128]{2,1,0:T(8,128)} %gather_fusion, f32[128,64,64]{2,1,0:T(8,128)} %copy.14), kind=kOutput, calls=%fused_computation.17 | convolution fusion | flops 805306368 | bytes 10485760 | tf_op jit(solution)/shard_map/sij,sjk->sik/dot_general | solution.py:22
  62.7 0.0 copy-start
  62.7 0.0 copy-start.2
  62.7 4.3 %fusion = f32[4,8192]{1,0:T(4,128)S(1)} fusion(f32[16,8,64,128]{3,2,1,0:T(8,128)S(1)} %bitcast.19, f32[128]{0:T(128)S(1)} %compare_convert_fusion, s32[128]{0:T(128)S(1)} %copy-done.3), kind=kOutput, calls=%fused_computation.1 | convolution fusion | flops 50332672 | bytes 4326400 | tf_op jit(solution)/shard_map/dot_general | solution.py:24
  67.1 0.1 reshape.28
  67.2 0.0 copy-done
  67.2 0.0 copy-done.2
  67.2 0.1 multiply_add_fusion
  67.3 0.0 copy-start.1
  67.3 1.0 fusion.3
  68.3 0.0 all-reduce.2.cloned.1.call-update
  68.3 86.9 %all-reduce.2.cloned.1.call-done = f32[128,128]{0,1:T(8,128)} async-done(((f32[128,128]{0,1:T(8,128)}), f32[128,128]{0,1:T(8,128)}) %all-reduce.2.cloned.1.call-update) | async-done | bytes 65552 | tf_op jit(solution)/shard_map/psum | solution.py:29
  155.3 1.6 copy.15
  (6 shorter events, 0.0 us)
Async XLA Ops:
  7.2 44.6 %all-gather.2.cloned.1.call-start = ((), (), s32[]{:S(2)}) async-start(), calls=%async_computation | async-start | bytes 2228224 | tf_op jit(solution)/shard_map/all_gather | solution.py:18
  7.9 147.4 %all-reduce.2.cloned.1.call-start = ((), (), s32[]{:S(2)}) async-start(), calls=%async_computation.1 | async-start | bytes 131072 | tf_op jit(solution)/shard_map/psum | solution.py:29
  9.9 5.2 %copy-start.4 = (s32[128]{0:T(128)S(1)}, s32[128]{0:T(128)}, u32[]{:S(2)}) copy-start(s32[128]{0:T(128)} %param.12) | copy-start | bytes 1540
  9.9 5.2 %copy-start.5 = (s32[128,1]{0,1:T(1,128)S(1)}, s32[128,1]{0,1:T(1,128)}, u32[]{:S(2)}) copy-start(s32[128,1]{0,1:T(1,128)} %param.11) | copy-start | bytes 1540
  56.1 6.6 %copy-start.3 = (s32[128]{0:T(128)S(1)}, s32[128]{0:T(128)}, u32[]{:S(2)}) copy-start(s32[128]{0:T(128)} %param.10) | copy-start | bytes 1540
  62.7 4.5 %copy-start = (f32[256,128]{1,0:T(8,128)S(1)}, f32[256,128]{1,0:T(8,128)}, u32[]{:S(2)}) copy-start(f32[256,128]{1,0:T(8,128)} %param.7) | copy-start | bytes 393220
  62.7 4.5 %copy-start.2 = (f32[256]{0:T(256)S(1)}, f32[256]{0:T(256)}, u32[]{:S(2)}) copy-start(f32[256]{0:T(256)} %param.8) | copy-start | bytes 3076
  67.3 89.5 %copy-start.1 = (f32[256,128]{1,0:T(8,128)}, f32[256,128]{1,0:T(8,128)S(1)}, u32[]{:S(2)}) copy-start(f32[256,128]{1,0:T(8,128)S(1)} %multiply_add_fusion) | copy-start | bytes 393220
Sparse Core Ops, SparseCore 0:
  10.2 41.5 all-gather.1
  68.5 86.7 all-reduce.1
where the time goes:
time: 164 us
  waiting for transfers between devices  124 us (76%)
  between operations  14.8 us (9%)
  local copies, waits for them, and re-layouts  12.5 us (8%)
  matrix products  11.9 us (7%)
    psum x1, waiting for transfers between devices, shards(): reduced = lax.psum(partial_term, 'row')  86.9 us
    all_gather x1, waiting for transfers between devices, shards(): gathered = lax.all_gather(own_blocks, 'row', axis=0, tiled=True)  36.7 us
    dot_general x1, matrix products, shards(): jnp.einsum('sij,sjk->sik', square_blocks, picked, precision=lax.Precision...  6.52 us
    reshape x1, local copies, waits for them, and re-layouts, shards(): square_blocks = tangent_blocks.reshape(CAP, B, B)  4.52 us
    gather x1, local copies, waits for them, and re-layouts, shards(): picked = gathered[owner_ids * BR_DEV + tile_offset]  4.35 us
    dot_general x1, matrix products, shards(): jnp.dot(row_select, products.reshape(CAP, B * MODES), precision=lax.Preci...  4.34 us
    unnamed x14, local copies, waits for them, and re-layouts  3.52 us
  transfers between devices with their start and end apart: 2, of which 2 were waited for; matrix products, arithmetic and copies ran while one was open for 4% of the time, Pallas kernels for 0%

commit v1 on v0

--- a/solution.py
+++ b/solution.py
@@ -7,6 +7,12 @@
 MODES = 128
 BR_DEV = 4
 CAP = 128
+
+
+def add_all(x, mesh_axis):
+    parts = lax.all_gather(x, mesh_axis, axis=0, tiled=False)
+    total = parts.sum(axis=0)
+    return total
 
 
 def shards(basis, springs, tangent_blocks, tile_rows, tile_owner, tile_offset, tile_count):
@@ -26,7 +32,7 @@
     partial_term = (
         jnp.einsum("rm,rn->mn", basis, stiff_image, precision=lax.Precision.HIGHEST) / dof_total
     )
-    reduced = lax.psum(partial_term, "row")
+    reduced = add_all(partial_term, "row")
     return (stiff_image, reduced)
 
 

time: 164 us -> 116 us (0.71)
  waiting for transfers between devices: 124 us -> 74.1 us
    psum x1 -> x0, waiting for transfers between devices: 86.9 us -> none  [shards(): reduced = lax.psum(partial_term, 'row')]
    all_gather x0 -> x1, waiting for transfers between devices: none -> 36.7 us  [add_all(): parts = lax.all_gather(x, mesh_axis, axis=0, tiled=False)]
    unnamed x14 -> x15, local copies, waits for them, and re-layouts: 3.52 us -> 4.09 us
  transfers between devices with their start and end apart: 2 -> 2, of which waited for: 2 -> 2; matrix products, arithmetic and copies ran while one was open for 4% -> 6% of each run, Pallas kernels for 0% -> 0%
where the time goes in v1:
time: 116 us; the launch traced here: 114 us
  waiting for transfers between devices  74.1 us (64%)
  between operations  14.8 us (13%)
  local copies, waits for them, and re-layouts  13.1 us (11%)
  matrix products  11.9 us (10%)
    all_gather x1, waiting for transfers between devices, add_all(): parts = lax.all_gather(x, mesh_axis, axis=0, tiled=False)  36.7 us
    all_gather x1, waiting for transfers between devices, shards(): gathered = lax.all_gather(own_blocks, 'row', axis=0, tiled=True)  36.7 us
    dot_general x1, matrix products, shards(): jnp.einsum('sij,sjk->sik', square_blocks, picked, precision=lax.Precision...  6.52 us
    reshape x1, local copies, waits for them, and re-layouts, shards(): square_blocks = tangent_blocks.reshape(CAP, B, B)  4.52 us
    gather x1, local copies, waits for them, and re-layouts, shards(): picked = gathered[owner_ids * BR_DEV + tile_offset]  4.35 us
    dot_general x1, matrix products, shards(): jnp.dot(row_select, products.reshape(CAP, B * MODES), precision=lax.Preci...  4.34 us
    unnamed x15, local copies, waits for them, and re-layouts  4.09 us
  transfers between devices with their start and end apart: 2, of which 2 were waited for; matrix products, arithmetic and copies ran while one was open for 6% of the time, Pallas kernels for 0%

profile of v1, /device:TPU:8, one launch (start us, length us, event | category | flops | bytes accessed | tf_op | source)
XLA Modules:
  0.0 114.2 jit_solution(9847418301706572811)
XLA Ops:
  7.2 0.0 all-gather.4.cloned.1.call-start
  7.2 0.7 all-gather.4.cloned.1.call-update
  7.9 0.0 all-gather.6.cloned.1.call-start
  7.9 1.9 %copy.11 = f32[128,4096]{0,1:T(8,128)S(1)} copy(f32[128,4096]{1,0:T(8,128)} %param.9) | data formatting | bytes 4194304 | tf_op args[2]
  9.9 0.0 copy-start.4
  9.9 0.0 copy-start.5
  9.9 4.5 %copy.12 = f32[128,64,64]{2,1,0:T(8,128)} copy(f32[128,64,64]{0,2,1:T(8,128)S(1)} %bitcast.25) | data formatting | bytes 4194304 | tf_op jit(solution)/shard_map/reshape | solution.py:22
  15.1 0.0 copy-done.4
  15.1 0.0 copy-done.5
  15.1 36.7 %all-gather.4.cloned.1.call-done = f32[64,64,128]{2,1,0:T(8,128)} async-done(((f32[4,64,128]{2,1,0:T(8,128)}), f32[64,64,128]{2,1,0:T(8,128)}) %all-gather.4.cloned.1.call-update) | async-done | bytes 2097168 | tf_op jit(solution)/shard_map/all_gather | solution.py:24
  51.8 4.4 %gather_fusion = f32[128,64,128]{2,1,0:T(8,128)} fusion(f32[64,64,128]{2,1,0:T(8,128)} %all-gather.4.cloned.1.call-done, s32[1024]{0:T(1024)S(1)} %pad_clamp_fusion), kind=kCustom, calls=%fused_computation | custom fusion | bytes 8389120 | tf_op jit(solution)/shard_map/gather | solution.py:25
  56.1 6.5 %fusion.9 = f32[128,128,64]{1,2,0:T(8,128)S(1)} fusion(f32[128,64,128]{2,1,0:T(8,128)} %gather_fusion, f32[128,64,64]{2,1,0:T(8,128)} %copy.12), kind=kOutput, calls=%fused_computation.18 | convolution fusion | flops 805306368 | bytes 10485760 | tf_op jit(solution)/shard_map/sij,sjk->sik/dot_general | solution.py:28
  62.7 0.0 copy-start
  62.7 0.0 copy-start.2
  62.7 4.3 %fusion = f32[4,8192]{1,0:T(4,128)S(1)} fusion(f32[16,8,64,128]{3,2,1,0:T(8,128)S(1)} %bitcast.24, f32[128]{0:T(128)S(1)} %compare_convert_fusion, s32[128]{0:T(128)S(1)} %copy-done.3), kind=kOutput, calls=%fused_computation.1 | convolution fusion | flops 50332672 | bytes 4326400 | tf_op jit(solution)/shard_map/dot_general | solution.py:30
  67.1 0.1 reshape.28
  67.2 0.1 multiply_add_fusion
  67.3 0.0 copy-start.1
  67.3 1.0 fusion.3
  68.3 0.0 all-gather.6.cloned.1.call-update
  68.3 36.7 %all-gather.6.cloned.1.call-done = f32[2048,128]{0,1:T(8,128)} async-done(((f32[128,128]{0,1:T(8,128)}), f32[2048,128]{0,1:T(8,128)}) %all-gather.6.cloned.1.call-update) | async-done | bytes 1048592 | tf_op jit(solution)/shard_map/all_gather | solution.py:13
  105.1 1.4 %copy.15 = f32[16,8,16,128]{3,2,1,0:T(8,128)S(1)} copy(f32[16,8,16,128]{3,1,2,0:T(8,128)} %bitcast.27) | data formatting | bytes 2097152
  106.5 0.2 bitcast_reduce_fusion
  106.6 0.7 copy.13
  (8 shorter events, 0.0 us)
Async XLA Ops:
  7.2 44.6 %all-gather.4.cloned.1.call-start = ((), (), s32[]{:S(2)}) async-start(), calls=%async_computation | async-start | bytes 2228224 | tf_op jit(solution)/shard_map/all_gather | solution.py:24
  7.9 97.2 %all-gather.6.cloned.1.call-start = ((), (), s32[]{:S(2)}) async-start(), calls=%async_computation.1 | async-start | bytes 1114112 | tf_op jit(solution)/shard_map/all_gather | solution.py:13
  9.9 5.2 %copy-start.4 = (s32[128]{0:T(128)S(1)}, s32[128]{0:T(128)}, u32[]{:S(2)}) copy-start(s32[128]{0:T(128)} %param.12) | copy-start | bytes 1540
  9.9 5.2 %copy-start.5 = (s32[128,1]{0,1:T(1,128)S(1)}, s32[128,1]{0,1:T(1,128)}, u32[]{:S(2)}) copy-start(s32[128,1]{0,1:T(1,128)} %param.11) | copy-start | bytes 1540
  56.1 6.6 %copy-start.3 = (s32[128]{0:T(128)S(1)}, s32[128]{0:T(128)}, u32[]{:S(2)}) copy-start(s32[128]{0:T(128)} %param.10) | copy-start | bytes 1540
  62.7 4.5 %copy-start = (f32[256,128]{1,0:T(8,128)S(1)}, f32[256,128]{1,0:T(8,128)}, u32[]{:S(2)}) copy-start(f32[256,128]{1,0:T(8,128)} %param.7) | copy-start | bytes 393220
  62.7 4.5 %copy-start.2 = (f32[256]{0:T(256)S(1)}, f32[256]{0:T(256)}, u32[]{:S(2)}) copy-start(f32[256]{0:T(256)} %param.8) | copy-start | bytes 3076
  67.3 40.1 %copy-start.1 = (f32[256,128]{1,0:T(8,128)}, f32[256,128]{1,0:T(8,128)S(1)}, u32[]{:S(2)}) copy-start(f32[256,128]{1,0:T(8,128)S(1)} %multiply_add_fusion) | copy-start | bytes 393220
Sparse Core Ops, SparseCore 0:
  10.2 41.5 all-gather.3
  68.5 36.5 all-gather.5
